TPU v7x, 32 devices: a whole 2x2x4 slice. The times are simulated.
32 devices in a mesh: grp: 2 (over x), dev: 16 (over z, y, core).
Axes of the slice: x: 2, y: 2, z: 4, core: 2. Of those that a mesh axis runs over, the one named last changes fastest.
Arguments:
- kv_pool: bfloat16 [768, 64, 512], P(('grp', 'dev')), parts along dimension 0, may hold values from -6 to 6
- block_table: int32 [32, 24], P(('grp', 'dev')), parts along dimension 0, may hold values from 0 to 383, as said below
- lengths: int32 [32], P(('grp', 'dev')), parts along dimension 0, may hold values from 1 to 1536, as said below
- queries: bfloat16 [2, 32, 16384], P(None, ('grp', 'dev')), parts along dimension 1, may hold values from -32 to 32
- new_kv: bfloat16 [2, 32, 512], P(None, ('grp', 'dev')), parts along dimension 1, may hold values from -8 to 8
- residual_in: bfloat16 [2, 32, 7168], P(None, ('grp', 'dev')), parts along dimension 1, may hold values from -8 to 8
- norm_gain: bfloat16 [7168], replicated, may hold values from 0.099609375 to 1.8984375
- out_weight: bfloat16 [16384, 7168], P('dev'), may hold values from -0.375 to 0.375
- gate_weight: bfloat16 [7168, 9216], P(None, 'dev'), may hold values from -0.0625 to 0.0625
- up_weight: bfloat16 [7168, 9216], P(None, 'dev'), may hold values from -0.0625 to 0.0625
- down_weight: bfloat16 [9216, 7168], P('dev'), may hold values from -0.0625 to 0.0625
Outputs:
- layer_out: float32 [2, 32, 7168], P(None, ('grp', 'dev')), parts along dimension 1
There are 2 independent parts, one for each index of `grp`. A program takes and returns all parts, laid end to end along the dimension named above; an argument that names none is the same for every part. Nothing has to cross between parts.
Inputs may be any that keep to these rules, and one draw needn't show every extreme that they name: `lengths`: one request of every serving group has exactly 1536 cached positions. `block_table`: request r is placed on device r: every entry of row r lies in that device's blocks, (r) * 24 to (r) * 24 + 23, and the requests of one device list each of its blocks exactly once.
All inputs are finite; a program needn't handle non-finite values.
Results may differ from a plain program's by a relative error of at most 0.0046.
Values may be sent and summed in bfloat16 or wider, within the bound.
A program may use at most 128 MiB of HBM per device.

v0:
```python
import jax
import jax.numpy as jnp
from jax import lax
from jax.sharding import PartitionSpec as P


def per_device(
    kv_pool,
    block_table,
    lengths,
    queries,
    new_kv,
    residual_in,
    norm_gain,
    out_weight,
    gate_weight,
    up_weight,
    down_weight,
):
    local_count = queries.shape[1]
    pool_blocks = kv_pool.shape[0]
    head_width = new_kv.shape[2] // 2
    head_count = queries.shape[2] // head_width
    model_width = residual_in.shape[2]
    cache_rows = kv_pool[block_table % pool_blocks].reshape(local_count, -1, 2 * head_width)
    cache_length = cache_rows.shape[1]
    visible = jnp.arange(cache_length, dtype=jnp.int32)[None, :] < lengths[:, None]
    scale_factor = head_width ** (-0.5)

    def attend(step_index):
        query_heads = queries[step_index].reshape(-1, head_count, head_width)
        cache_scores = (
            jnp.einsum(
                "rhd,rld->rhl",
                query_heads,
                cache_rows[:, :, :head_width],
                preferred_element_type=jnp.float32,
            )
            * scale_factor
        )
        cache_scores = jnp.where(visible[:, None, :], cache_scores, -jnp.inf)
        fresh_scores = (
            jnp.einsum(
                "rhd,srd->rhs",
                query_heads,
                new_kv[:, :, :head_width],
                preferred_element_type=jnp.float32,
            )
            * scale_factor
        )
        fresh_visible = jnp.arange(new_kv.shape[0]) <= step_index
        fresh_scores = jnp.where(fresh_visible[None, None, :], fresh_scores, -jnp.inf)
        largest = jnp.maximum(jnp.max(cache_scores, axis=-1), jnp.max(fresh_scores, axis=-1))[
            ..., None
        ]
        cache_weights = jnp.exp(cache_scores - largest)
        fresh_weights = jnp.exp(fresh_scores - largest)
        denominator = jnp.sum(cache_weights, axis=-1, keepdims=True) + jnp.sum(
            fresh_weights, axis=-1, keepdims=True
        )
        cache_probs = (cache_weights / denominator).astype(jnp.bfloat16)
        fresh_probs = (fresh_weights / denominator).astype(jnp.bfloat16)
        attended = jnp.einsum(
            "rhl,rld->rhd",
            cache_probs,
            cache_rows[:, :, head_width:],
            preferred_element_type=jnp.float32,
        )
        attended = attended + jnp.einsum(
            "rhs,srd->rhd",
            fresh_probs,
            new_kv[:, :, head_width:],
            preferred_element_type=jnp.float32,
        )
        return attended.astype(jnp.bfloat16).reshape(-1, head_count * head_width)

    step_list = list(range(queries.shape[0]))
    attended = jnp.concatenate([attend(step_index) for step_index in step_list], 0)
    residual_rows = jnp.concatenate([residual_in[step_index] for step_index in step_list], 0)
    head_slices = lax.all_to_all(attended, "dev", split_axis=1, concat_axis=0, tiled=True)
    rows_now = head_slices
    summed = lax.psum_scatter(
        jnp.dot(rows_now, out_weight, preferred_element_type=jnp.float32),
        "dev",
        scatter_dimension=0,
        tiled=True,
    )
    state = residual_rows.astype(jnp.float32) + summed
    scale_rows = lax.rsqrt(jnp.mean(state * state, axis=-1, keepdims=True) + 1e-06)
    normed = (state * scale_rows * norm_gain.astype(jnp.float32)).astype(jnp.bfloat16)
    row_piece = lax.all_gather(normed, "dev", axis=0, tiled=True)
    gate_out = jnp.dot(row_piece, gate_weight, preferred_element_type=jnp.float32)
    up_out = jnp.dot(row_piece, up_weight, preferred_element_type=jnp.float32)
    hidden_units = (jax.nn.silu(gate_out) * up_out).astype(jnp.bfloat16)
    rows_now = hidden_units
    finished = state + lax.psum_scatter(
        jnp.dot(rows_now, down_weight, preferred_element_type=jnp.float32),
        "dev",
        scatter_dimension=0,
        tiled=True,
    )
    return finished.reshape(len(step_list), local_count, model_width)


def solution(mesh):
    placed = (
        P(("grp", "dev"), None, None),
        P(("grp", "dev"), None),
        P(("grp", "dev")),
        P(None, ("grp", "dev"), None),
        P(None, ("grp", "dev"), None),
        P(None, ("grp", "dev"), None),
        P(),
        P("dev", None),
        P(None, "dev"),
        P(None, "dev"),
        P("dev", None),
    )
    return jax.shard_map(
        per_device,
        mesh=mesh,
        in_specs=placed,
        out_specs=P(None, ("grp", "dev"), None),
        check_vma=False,
    )
```

profile of v0, /device:TPU:0, one launch (start us, length us, event | category | flops | bytes accessed | tf_op | source)
XLA Modules:
  0.0 264.6 jit_solution(15903156074523500101)
XLA Ops:
  6.6 0.8 fusion.34
  7.4 1.3 slice_reduce_fusion.1
  9.3 0.6 gather_fusion
  10.0 0.5 fusion.42
  10.5 0.8 fusion.43
  11.3 0.2 fusion.10
  11.6 0.3 fusion.9
  11.9 0.9 fusion.3
  12.8 0.5 fusion.40
  13.3 0.1 fusion.41
  13.4 0.2 fusion.11
  13.7 0.3 fusion.8
  14.0 0.2 fusion.4
  14.3 0.2 pad_maximum_fusion
  14.4 14.1 %all_to_all.16 = bf16[2,16,1024]{2,0,1:T(2,128)(2,1)S(1)} all-to-all(bf16[2,16,1024]{2,0,1:T(2,128)(2,1)S(1)} %pad_maximum_fusion), channel_id=1, replica_groups=mesh['grp'=2,'dev'=16] {'dev'}, dimensions={1} | all-to-all | bytes 131072 | tf_op jit(solution)/shard_map/all_to_all | solution.py:80
  28.5 0.0 copy-start.1
  28.6 0.0 copy-start.4
  28.6 8.8 %fusion.44 = f32[32,7168]{1,0:T(8,128)} fusion(bf16[32,1024]{1,0:T(8,128)(2,1)S(1)} %all_to_all.14, bf16[1024,7168]{1,0:T(8,128)(2,1)} %param.18), kind=kOutput, calls=%fused_computation.78 | convolution fusion | flops 469762048 | bytes 15663104 | tf_op jit(solution)/shard_map/dot_general | solution.py:83
  37.4 0.0 all-reduce.5.cloned.1.call-update
  37.4 0.0 all-reduce.7.cloned.1.call-start
  37.5 0.6 dynamic-slice
  38.8 88.0 %all-reduce.5.cloned.1.call-done = f32[32,7168]{1,0:T(8,128)} async-done(((f32[32,7168]{1,0:T(8,128)}), f32[32,7168]{1,0:T(8,128)}) %all-reduce.5.cloned.1.call-update) | async-done | bytes 917520
  126.8 1.2 multiply_reduce_fusion
  128.0 0.1 fusion.23
  128.1 21.9 %all-gather = bf16[16,2,7168]{2,1,0:T(2,128)(2,1)S(1)} all-gather(bf16[1,2,7168]{2,1,0:T(2,128)(2,1)S(1)} %fusion.23), channel_id=1, replica_groups=mesh['grp'=2,'dev'=16] {'dev'}, dimensions={0}, use_global_device_ids=true | all-gather | bytes 487424 | tf_op jit(solution)/shard_map/all_gather | solution.py:91
  150.0 0.2 reshape.204
  150.2 5.8 %fusion.45 = f32[32,576]{1,0:T(8,128)S(1)} fusion(bf16[32,7168]{1,0:T(8,128)(2,1)S(1)} %reshape.204, bf16[7168,576]{0,1:T(8,128)(2,1)} %param.19), kind=kOutput, calls=%fused_computation.79 | convolution fusion | flops 264241152 | bytes 8790016 | tf_op jit(solution)/shard_map/dot_general | solution.py:92
  156.0 11.0 %fusion.7 = f32[32,7168]{1,0:T(8,128)} fusion(bf16[576,7168]{1,0:T(8,128)(2,1)} %param.21, bf16[32,7168]{1,0:T(8,128)(2,1)S(1)} %reshape.204, bf16[7168,576]{0,1:T(8,128)(2,1)} %param.20, f32[32,576]{1,0:T(8,128)S(1)} %fusion.45), kind=kOutput, calls=%fused_computation.15 | convolution fusion | flops 528592896 | bytes 17965056 | tf_op jit(solution)/shard_map/dot_general | solution.py:97
  166.9 0.0 all-reduce.7.cloned.1.call-update
  167.0 89.2 %all-reduce.7.cloned.1.call-done = f32[32,7168]{1,0:T(8,128)} async-done(((f32[32,7168]{1,0:T(8,128)}), f32[32,7168]{1,0:T(8,128)}) %all-reduce.7.cloned.1.call-update) | async-done | bytes 917520
  256.2 1.0 fusion.21
  257.1 0.7 copy.18
  (27 shorter events, 0.3 us)
Async XLA Ops:
  6.5 2.8 %copy-start = (bf16[24,64,512]{2,1,0:T(8,128)(2,1)S(1)}, bf16[24,64,512]{2,1,0:T(8,128)(2,1)}, u32[]{:S(2)}) copy-start(bf16[24,64,512]{2,1,0:T(8,128)(2,1)} %param.11) | copy-start | bytes 4718596
  6.5 6.7 %copy-start.3 = (bf16[2,1,512]{2,0,1:T(2,128)(2,1)S(1)}, bf16[2,1,512]{2,0,1:T(2,128)(2,1)}, u32[]{:S(2)}) copy-start(bf16[2,1,512]{2,0,1:T(2,128)(2,1)} %param.15) | copy-start | bytes 6148
  6.5 120.3 %all-reduce.5.cloned.1.call-start = ((), (), s32[]{:S(2)}) async-start(), calls=%async_computation.1 | async-start | bytes 1835008
  28.5 8.9 %copy-start.1 = (bf16[2,1,7168]{2,0,1:T(2,128)(2,1)S(1)}, bf16[2,1,7168]{2,0,1:T(2,128)(2,1)}, u32[]{:S(2)}) copy-start(bf16[2,1,7168]{2,0,1:T(2,128)(2,1)} %param.16) | copy-start | bytes 86020
  28.6 8.9 %copy-start.2 = (bf16[7168]{0:T(1024)(128)(2,1)S(1)}, bf16[7168]{0:T(1024)(128)(2,1)}, u32[]{:S(2)}) copy-start(bf16[7168]{0:T(1024)(128)(2,1)} %param.17) | copy-start | bytes 43012
  28.6 9.0 %copy-start.4 = (u32[32]{0:T(128)S(1)}, u32[32]{0:T(128)}, u32[]{:S(2)}) copy-start(u32[32]{0:T(128)} %constant.40) | copy-start | bytes 388
  37.4 218.8 %all-reduce.7.cloned.1.call-start = ((), (), s32[]{:S(2)}) async-start(), calls=%async_computation.2 | async-start | bytes 1835008
Sparse Core Ops, SparseCore 0:
  37.5 89.2 all-reduce.4
  167.1 89.0 all-reduce.6
where the time goes:
time: 265 us
  waiting for transfers between devices  177 us (67%)
  blocking collectives  36 us (14%)
  matrix products  29.2 us (11%)
  between operations  14.9 us (6%)
  other arithmetic  3.75 us (1%)
  local copies, waits for them, and re-layouts  3.54 us (1%)
    unnamed x4, waiting for transfers between devices  177 us
    all_gather x1, blocking collectives, per_device(): row_piece = lax.all_gather(normed, 'dev', axis=0, tiled=True)  21.9 us
    all_to_all x1, blocking collectives, per_device(): lax.all_to_all(attended, 'dev', split_axis=1, concat_axis=0, tiled=True)  14.1 us
    dot_general x1, matrix products, per_device(): jnp.dot(rows_now, down_weight, preferred_element_type=jnp.float32)  11 us
    dot_general x1, matrix products, per_device(): jnp.dot(rows_now, out_weight, preferred_element_type=jnp.float32)  8.78 us
    dot_general x1, matrix products, per_device(): jnp.dot(row_piece, gate_weight, preferred_element_type=jnp.float32)  5.8 us
  transfers between devices with their start and end apart: 2, of which 2 were waited for; matrix products, arithmetic and copies ran while one was open for 0% of the time, Pallas kernels for 0%

commit v1 on v0

v1 whole, which is shorter than its diff:
```python
import functools

import jax
import jax.numpy as jnp
from jax import lax
from jax.experimental import pallas as pl
from jax.experimental.pallas import tpu as pltpu
from jax.sharding import PartitionSpec as P

F32 = jnp.float32
BF16 = jnp.bfloat16
MESH = pl.DeviceIdType.MESH
WIDE = 1024


def layer_kernel(
    n,
    table_ref,
    length_ref,
    q_ref,
    fresh_ref,
    res_ref,
    gain_ref,
    kv_hbm,
    wo_hbm,
    wg_hbm,
    wu_hbm,
    wd_hbm,
    out_ref,
    kv,
    wo,
    wg,
    wu,
    wd,
    att,
    att_send,
    att_recv,
    att_wide,
    lhs,
    part,
    send1,
    recv1,
    acc1,
    send2,
    recv2,
    acc2,
    send3,
    recv3,
    state,
    rows_all,
    rows_wide,
    normed,
    kv_sem,
    w_sem,
    att_ssem,
    att_rsem,
    s1_sem,
    r1_sem,
    s2_sem,
    r2_sem,
    s3_sem,
    r3_sem,
    gz_ssem,
    gz_rsem,
    gy_ssem,
    gy_rsem,
    gc_ssem,
    gc_rsem,
):
    me = lax.axis_index("dev")
    nz = n // 4
    core, y, z = lax.rem(me, 2), lax.rem(me // 2, 2), me // 4
    chunks = state.shape[0]
    heads_dev = lhs.shape[1] // 256
    rows = 2 * n
    width = chunks * WIDE

    def slot_of(i):
        return lax.rem(i, 2) * (n // 2) + lax.rem(i // 2, 2) * nz + i // 4

    my_slot = slot_of(me)
    twin = me + 1 - 2 * core
    y_peer = me + 2 - 4 * y

    def z_peer(off):
        other = lax.rem(z + off, nz)
        return other, other * 4 + y * 2 + core

    kv_copy = pltpu.make_async_copy(kv_hbm, kv, kv_sem)
    kv_copy.start()

    def columns(c):
        return pl.ds(c * WIDE, WIDE)

    wo_copies = [
        pltpu.make_async_copy(wo_hbm.at[:, columns(c)], wo.at[:, columns(c)], w_sem.at[0, c])
        for c in range(chunks)
    ]
    wg_copies = [
        pltpu.make_async_copy(wg_hbm.at[columns(c)], wg.at[columns(c)], w_sem.at[1, c])
        for c in range(chunks)
    ]
    wu_copies = [
        pltpu.make_async_copy(wu_hbm.at[columns(c)], wu.at[columns(c)], w_sem.at[2, c])
        for c in range(chunks)
    ]
    wd_copies = [
        pltpu.make_async_copy(wd_hbm.at[:, columns(c)], wd.at[:, columns(c)], w_sem.at[3, c])
        for c in range(chunks)
    ]
    for copy in wo_copies:
        copy.start()
    for pair in zip(wg_copies, wu_copies):
        for copy in pair:
            copy.start()
    for copy in wd_copies:
        copy.start()

    barrier = pltpu.get_barrier_semaphore()

    def greet(off, carry):
        pl.semaphore_signal(
            barrier, inc=1, device_id={"dev": lax.rem(me + off, n)}, device_id_type=MESH
        )
        return carry

    lax.fori_loop(1, n, greet, 0)

    positions = kv.shape[0]
    blocks = table_ref.shape[1]
    block_rows = positions // blocks
    place = lax.broadcasted_iota(jnp.int32, (1, positions), 1)
    block_of = place // block_rows
    order = jnp.zeros((1, positions), jnp.int32)
    for j in range(blocks):
        order = jnp.where(block_of == lax.rem(table_ref[0, j], blocks), j, order)
    position = order * block_rows + (place - block_of * block_rows)
    visible = position < length_ref[0]

    q = q_ref[...]
    q_rows = q.shape[0]
    contract_last = (((1,), (1,)), ((), ()))
    fresh = fresh_ref[...]
    fresh_scores = (
        lax.dot_general(q, fresh[:, :256], contract_last, preferred_element_type=F32) * 0.0625
    )
    step_of_row = lax.rem(lax.broadcasted_iota(jnp.int32, (q_rows, 16), 0), 2)
    fresh_step = lax.broadcasted_iota(jnp.int32, (q_rows, 16), 1)
    fresh_scores = jnp.where(fresh_step <= step_of_row, fresh_scores, -jnp.inf)
    kv_copy.wait()
    scores = (
        lax.dot_general(q, kv[:, :256], contract_last, preferred_element_type=F32) * 0.0625
    )
    scores = jnp.where(visible, scores, -jnp.inf)
    largest = jnp.maximum(
        jnp.max(scores, axis=1, keepdims=True), jnp.max(fresh_scores, axis=1, keepdims=True)
    )
    weights = jnp.exp(scores - largest)
    fresh_weights = jnp.exp(fresh_scores - largest)
    total = jnp.sum(weights, axis=1, keepdims=True) + jnp.sum(
        fresh_weights, axis=1, keepdims=True
    )
    probs = (weights / total).astype(BF16)
    fresh_probs = (fresh_weights / total).astype(BF16)
    attended = jnp.dot(probs, kv[:, 256:], preferred_element_type=F32) + jnp.dot(
        fresh_probs, fresh[:, 256:], preferred_element_type=F32
    )
    if heads_dev < 4:
        att[...] = jnp.zeros_like(att)
    for h in range(heads_dev):
        for half in range(2):
            att[pl.ds(h * 2 + half, rows, stride=8), :] = attended[
                h * rows : (h + 1) * rows, half * 128 : (half + 1) * 128
            ]
    att_send[...] = att[...].astype(BF16).reshape(att_send.shape)

    pl.semaphore_wait(barrier, n - 1)

    def att_copy(off):
        peer = lax.rem(me + off, n)
        return pltpu.make_async_remote_copy(
            src_ref=att_send.at[peer],
            dst_ref=att_recv.at[my_slot],
            send_sem=att_ssem.at[off],
            recv_sem=att_rsem.at[my_slot],
            device_id={"dev": peer},
            device_id_type=MESH,
        )

    def start_att(off, carry):
        att_copy(off).start()
        return carry

    lax.fori_loop(1, n, start_att, 0)
    att_recv[my_slot] = att_send[me]

    def wait_att(off, carry):
        source = slot_of(lax.rem(me + off, n))
        pltpu.make_async_remote_copy(
            src_ref=att_send.at[0],
            dst_ref=att_recv.at[source],
            send_sem=att_ssem.at[off],
            recv_sem=att_rsem.at[source],
            device_id={"dev": twin},
            device_id_type=MESH,
        ).wait_recv()
        return carry

    lax.fori_loop(1, n, wait_att, 0)
    att_wide[...] = att_recv[...].astype(F32).reshape(att_wide.shape)
    for k in range(2 * heads_dev):
        lhs[:, k * 128 : (k + 1) * 128] = att_wide[pl.ds(k, rows, stride=8), :].astype(BF16)

    half_rows, quarter_rows = n * 8, n * 4
    group = (chunks + 6) // 7

    def move(src, dst, ssem, rsem, peer):
        return pltpu.make_async_remote_copy(
            src_ref=src,
            dst_ref=dst,
            send_sem=ssem,
            recv_sem=rsem,
            device_id={"dev": peer},
            device_id_type=MESH,
        )

    def reduce_rows(turn, product):
        def to_twin(c):
            return move(
                send1.at[turn, c], recv1.at[turn, c], s1_sem.at[turn, c], r1_sem.at[turn, c], twin
            )

        def to_y(c):
            return move(
                send2.at[turn, c], recv2.at[turn, c], s2_sem.at[turn, c], r2_sem.at[turn, c], y_peer
            )

        def to_z(c, off):
            other, peer = z_peer(off)
            return move(
                send3.at[turn, c, other],
                recv3.at[turn, c, off],
                s3_sem.at[turn, c, off],
                r3_sem.at[turn, c, off],
                peer,
            )

        def first(c):
            tile = product(c)
            for j in range(8):
                part[c, pl.ds(j, rows, stride=8), :] = tile[:, j * 128 : (j + 1) * 128]
            away = pl.multiple_of((1 - core) * half_rows, half_rows)
            send1[turn, c] = part[c, pl.ds(away, half_rows), :].astype(BF16)
            to_twin(c).start()

        def second(c):
            to_twin(c).wait_recv()
            home = pl.multiple_of(core * half_rows, half_rows)
            acc1[c] = part[c, pl.ds(home, half_rows), :] + recv1[turn, c].astype(F32)
            away = pl.multiple_of((1 - y) * quarter_rows, quarter_rows)
            send2[turn, c] = acc1[c, pl.ds(away, quarter_rows), :].astype(BF16)
            to_y(c).start()

        def third(c):
            to_y(c).wait_recv()
            home = pl.multiple_of(y * quarter_rows, quarter_rows)
            held = acc1[c, pl.ds(home, quarter_rows), :] + recv2[turn, c].astype(F32)
            held = held.reshape(nz, 16, 128)
            acc2[c] = held
            send3[turn, c] = held.astype(BF16)
            for off in range(1, nz):
                to_z(c, off).start()

        for step in range(chunks + 2):
            if step < chunks:
                first(step)
            if 0 <= step - 1 < chunks:
                second(step - 1)
            if 0 <= step - 2 < chunks:
                third(step - 2)
        sums = []
        for c in range(chunks):
            total = acc2[c, z]
            for off in range(1, nz):
                to_z(c, off).wait_recv()
                total = total + recv3[turn, c, off].astype(F32)
            sums.append(total)

        def finish():
            for c in range(chunks):
                to_twin(c).wait_send()
                to_y(c).wait_send()
                for off in range(1, nz):
                    to_z(c, off).wait_send()

        return sums, finish

    def project(c):
        wo_copies[c].wait()
        return jnp.dot(lhs[...], wo[:, columns(c)], preferred_element_type=F32)

    sums, finish_first = reduce_rows(0, project)
    square = jnp.zeros((16, 128), F32)
    for c in range(chunks):
        row = res_ref[c].astype(F32) + sums[c]
        state[c] = row
        square = square + row * row
    scale0 = lax.rsqrt(jnp.sum(square[:8], keepdims=True) / width + 1e-06)
    scale1 = lax.rsqrt(jnp.sum(square[8:], keepdims=True) / width + 1e-06)
    scale = jnp.concatenate(
        [jnp.broadcast_to(scale0, (8, 128)), jnp.broadcast_to(scale1, (8, 128))], axis=0
    )

    my_rows = pl.multiple_of(my_slot * 16, 16)
    y_rows = pl.multiple_of((core * 2 + y) * quarter_rows, quarter_rows)
    core_rows = pl.multiple_of(core * half_rows, half_rows)
    y_in_rows = pl.multiple_of((core * 2 + 1 - y) * quarter_rows, quarter_rows)
    core_in_rows = pl.multiple_of((1 - core) * half_rows, half_rows)

    def spread_z(c, off):
        block = rows_all.at[c, pl.ds(my_rows, 16)]
        return move(block, block, gz_ssem.at[c, off], gz_rsem.at[c, off], z_peer(off)[1])

    def landed_z(c, off):
        source = lax.rem(z + nz - off, nz)
        block = rows_all.at[c, pl.ds(pl.multiple_of(y_rows + source * 16, 16), 16)]
        return move(block, block, gz_ssem.at[c, off], gz_rsem.at[c, off], z_peer(off)[1])

    def spread_y(c, start):
        block = rows_all.at[c, pl.ds(start, quarter_rows)]
        return move(block, block, gy_ssem.at[c], gy_rsem.at[c], y_peer)

    def spread_core(c, start):
        block = rows_all.at[c, pl.ds(start, half_rows)]
        return move(block, block, gc_ssem.at[c], gc_rsem.at[c], twin)

    for c in range(chunks):
        gain = gain_ref[c].astype(F32)
        gain = jnp.concatenate([gain, gain], axis=0)
        rows_all[c, pl.ds(my_rows, 16), :] = (state[c] * scale * gain).astype(BF16)
        for off in range(1, nz):
            spread_z(c, off).start()

    gate = jnp.zeros((rows, wg.shape[1]), F32)
    up = jnp.zeros((rows, wg.shape[1]), F32)
    for step in range(chunks + 2):
        if step < chunks:
            for off in range(1, nz):
                landed_z(step, off).wait_recv()
            spread_y(step, y_rows).start()
        if 0 <= step - 1 < chunks:
            c = step - 1
            spread_y(c, y_in_rows).wait_recv()
            spread_core(c, core_rows).start()
        if 0 <= step - 2 < chunks:
            c = step - 2
            spread_core(c, core_in_rows).wait_recv()
            rows_wide[...] = rows_all[c].astype(F32)
            for j in range(8):
                normed[:, j * 128 : (j + 1) * 128] = rows_wide[
                    pl.ds(j, rows, stride=8), :
                ].astype(BF16)
            held = normed[...]
            wg_copies[c].wait()
            wu_copies[c].wait()
            gate = gate + jnp.dot(held, wg[columns(c), :], preferred_element_type=F32)
            up = up + jnp.dot(held, wu[columns(c), :], preferred_element_type=F32)

    hidden = (gate / (1.0 + jnp.exp(-gate)) * up).astype(BF16)

    def down(c):
        wd_copies[c].wait()
        return jnp.dot(hidden, wd[:, columns(c)], preferred_element_type=F32)

    sums, finish_second = reduce_rows(1, down)
    for c in range(chunks):
        out_ref[c] = state[c] + sums[c]

    def drain_att(off, carry):
        att_copy(off).wait_send()
        return carry

    lax.fori_loop(1, n, drain_att, 0)
    finish_first()
    finish_second()
    for c in range(chunks):
        for off in range(1, nz):
            spread_z(c, off).wait_send()
        spread_y(c, y_rows).wait_send()
        spread_core(c, core_rows).wait_send()


def per_device(
    n,
    kv_pool,
    block_table,
    lengths,
    queries,
    new_kv,
    residual_in,
    norm_gain,
    out_weight,
    gate_weight,
    up_weight,
    down_weight,
):
    steps = queries.shape[0]
    head_width = new_kv.shape[2] // 2
    head_count = queries.shape[2] // head_width
    heads_dev = head_count // n
    width = residual_in.shape[2]
    chunks = width // WIDE
    units = gate_weight.shape[1]
    nz = n // 4
    positions = kv_pool.shape[0] * kv_pool.shape[1]

    q = (
        queries.reshape(steps, n, heads_dev, head_width)
        .transpose(2, 1, 0, 3)
        .reshape(head_count * steps, head_width)
    )
    fresh = jnp.pad(new_kv.reshape(steps, -1), ((0, 16 - steps), (0, 0)))
    residual = (
        residual_in.reshape(steps, chunks, 8, 128)
        .transpose(1, 0, 2, 3)
        .reshape(chunks, 8 * steps, 128)
    )
    gain = norm_gain.reshape(chunks, 8, 128)
    cache = kv_pool.reshape(positions, 2 * head_width)

    vmem = pl.BlockSpec(memory_space=pltpu.VMEM)
    smem = pl.BlockSpec(memory_space=pltpu.SMEM)
    hbm = pl.BlockSpec(memory_space=pl.ANY)
    dma = pltpu.SemaphoreType.DMA
    out = pl.pallas_call(
        functools.partial(layer_kernel, n),
        out_shape=jax.ShapeDtypeStruct((chunks, 16, 128), F32),
        in_specs=[smem, smem, vmem, vmem, vmem, vmem] + [hbm] * 5,
        out_specs=vmem,
        scratch_shapes=[
            pltpu.VMEM((positions, 2 * head_width), BF16),
            pltpu.VMEM(out_weight.shape, BF16),
            pltpu.VMEM(gate_weight.shape, BF16),
            pltpu.VMEM(up_weight.shape, BF16),
            pltpu.VMEM(down_weight.shape, BF16),
            pltpu.VMEM((n * 16, 128), F32),
            pltpu.VMEM((n, 16, 128), BF16),
            pltpu.VMEM((n, 16, 128), BF16),
            pltpu.VMEM((n * 16, 128), F32),
            pltpu.VMEM((2 * n, heads_dev * head_width), BF16),
            pltpu.VMEM((chunks, n * 16, 128), F32),
            pltpu.VMEM((2, chunks, n * 8, 128), BF16),
            pltpu.VMEM((2, chunks, n * 8, 128), BF16),
            pltpu.VMEM((chunks, n * 8, 128), F32),
            pltpu.VMEM((2, chunks, n * 4, 128), BF16),
            pltpu.VMEM((2, chunks, n * 4, 128), BF16),
            pltpu.VMEM((chunks, nz, 16, 128), F32),
            pltpu.VMEM((2, chunks, nz, 16, 128), BF16),
            pltpu.VMEM((2, chunks, nz, 16, 128), BF16),
            pltpu.VMEM((chunks, 16, 128), F32),
            pltpu.VMEM((chunks, n * 16, 128), BF16),
            pltpu.VMEM((n * 16, 128), F32),
            pltpu.VMEM((2 * n, WIDE), BF16),
            dma(()),
            dma((4, chunks)),
            dma((n,)),
            dma((n,)),
            dma((2, chunks)),
            dma((2, chunks)),
            dma((2, chunks)),
            dma((2, chunks)),
            dma((2, chunks, nz)),
            dma((2, chunks, nz)),
            dma((chunks, nz)),
            dma((chunks, nz)),
            dma((chunks,)),
            dma((chunks,)),
            dma((chunks,)),
            dma((chunks,)),
        ],
        compiler_params=pltpu.CompilerParams(
            collective_id=0, has_side_effects=True, vmem_limit_bytes=60 * 1024 * 1024
        ),
        cost_estimate=pl.CostEstimate(
            flops=2 * 2 * n * (out_weight.size + 3 * gate_weight.size),
            bytes_accessed=2 * (out_weight.size + 3 * gate_weight.size + cache.size),
            transcendentals=0,
        ),
        name="decode_layer",
    )(
        block_table,
        lengths,
        q,
        fresh,
        residual,
        gain,
        cache,
        out_weight,
        gate_weight,
        up_weight,
        down_weight,
    )
    return (
        out.reshape(chunks, steps, 8, 128).transpose(1, 0, 2, 3).reshape(steps, 1, width)
    )


def solution(mesh):
    placed = (
        P(("grp", "dev"), None, None),
        P(("grp", "dev"), None),
        P(("grp", "dev")),
        P(None, ("grp", "dev"), None),
        P(None, ("grp", "dev"), None),
        P(None, ("grp", "dev"), None),
        P(),
        P("dev", None),
        P(None, "dev"),
        P(None, "dev"),
        P("dev", None),
    )
    return jax.shard_map(
        functools.partial(per_device, mesh.shape["dev"]),
        mesh=mesh,
        in_specs=placed,
        out_specs=P(None, ("grp", "dev"), None),
        check_vma=False,
    )
```

time: 265 us -> 108 us (0.41)
  waiting for transfers between devices: 177 us -> 0 us
  Pallas kernels: 0 us -> 76.2 us
  blocking collectives: 36 us -> 0 us
  matrix products: 29.2 us -> 0 us
  local copies, waits for them, and re-layouts: 3.54 us -> 30.5 us
  between operations: 14.9 us -> 0.67 us
  other arithmetic: 3.75 us -> 0 us
    unnamed x4 -> x0, waiting for transfers between devices: 177 us -> none
    pallas_call x0 -> x1, Pallas kernels: none -> 76.2 us  [per_device(): pl.pallas_call(functools.partial(layer_kernel, n), out_shape=jax.ShapeDty...]
    dot_general x11 -> x0, matrix products: 29.2 us -> none  [the longest x1 11 us: per_device(): jnp.dot(rows_now, down_weight, preferred_element_type=jnp.float32)]
    unnamed x12 -> x2, local copies, waits for them, and re-layouts: 0.78 us -> 24.8 us
    all_gather x1 -> x0, blocking collectives: 21.9 us -> none  [per_device(): row_piece = lax.all_gather(normed, 'dev', axis=0, tiled=True)]
    all_to_all x1 -> x0, blocking collectives: 14.1 us -> none  [per_device(): lax.all_to_all(attended, 'dev', split_axis=1, concat_axis=0, tiled=True)]
  transfers between devices with their start and end apart: 2 -> 0, of which waited for: 2 -> 0; matrix products, arithmetic and copies ran while one was open for 0% -> 0% of each run, Pallas kernels for 0% -> 0%
where the time goes in v1:
time: 108 us; the launch traced here: 107 us
  Pallas kernels  76.2 us (71%)
  local copies, waits for them, and re-layouts  30.5 us (28%)
    pallas_call x1, Pallas kernels, per_device(): pl.pallas_call(functools.partial(layer_kernel, n), out_shape=jax.ShapeDty...  76.2 us
    unnamed x2, local copies, waits for them, and re-layouts  24.8 us

profile of v1, /device:TPU:0, one launch (start us, length us, event | category | flops | bytes accessed | tf_op | source)
XLA Modules:
  0.0 107.4 jit_solution(12977602572265654366)
XLA Ops:
  0.7 1.3 %pad.4.fresh_ref = bf16[16,512]{1,0:T(8,128)(2,1)} pad(bf16[2,512]{1,0:T(2,128)(2,1)} %bitcast.28, bf16[]{:T(256)} %constant.2.clone.1), padding=0_14x0_0 | pad | bytes 18434 | tf_op jit(solution)/shard_map/jit(_pad)/pad | solution.py:422
  1.9 1.4 %copy_bitcast_fusion.2.res_ref = bf16[7,16,128]{2,1,0:T(8,128)(2,1)} fusion(bf16[1,2,56,128]{3,1,2,0:T(2,128)(2,1)} %bitcast.26), kind=kLoop, calls=%fused_computation.2 | loop fusion | bytes 57344 | tf_op jit(solution)/shard_map/reshape | solution.py:426
  3.3 0.9 reshape.27
  4.2 0.1 copy.22
  4.3 0.6 reshape.28.q_ref
  4.9 12.4 %copy.14.wg_hbm = bf16[7168,576]{1,0:T(8,128)(2,1)} copy(bf16[7168,576]{0,1:T(8,128)(2,1)} %param.19) | data formatting | bytes 16515072 | tf_op args[8]
  17.3 12.4 %copy.15.wu_hbm = bf16[7168,576]{1,0:T(8,128)(2,1)} copy(bf16[7168,576]{0,1:T(8,128)(2,1)} %param.20) | data formatting | bytes 16515072 | tf_op args[9]
  29.7 76.2 %decode_layer.1 = f32[7,16,128]{2,1,0:T(8,128)} custom-call(s32[1,24]{1,0:T(1,128)} %table_ref.1, s32[1]{0:T(128)S(6)} %copy.23.length_ref, bf16[128,256]{1,0:T(8,128)(2,1)} %reshape.28.q_ref, bf16[16,512]{1,0:T(8,128)(2,1)} %pad.4.fresh_ref, bf16[7,16,128]{2,1,0:T(8,128)(2,1)} %copy_bitcast_fusion.2.res_ref, bf16[7,8,128]{2,1,0:T(8,128)(2,1)} %bitcast.27, ...), custom_call_target="tpu_custom_call" | custom-call | flops 1262485504 | bytes 41025536 | tf_op jit(solution)/shard_map/decode_layer/pallas_call | solution.py:435
  105.9 1.4 %copy.16 = f32[2,7,8,128]{3,2,1,0:T(8,128)} copy(f32[2,7,8,128]{3,2,0,1:T(8,128)} %bitcast.25) | data formatting | bytes 114688 | tf_op jit(solution)/shard_map/transpose | solution.py:504

commit v2 on v1

--- a/solution.py
+++ b/solution.py
@@ -10,6 +10,8 @@
 F32 = jnp.float32
 BF16 = jnp.bfloat16
 MESH = pl.DeviceIdType.MESH
+RS_GROUPS = 2
+AG_GROUPS = 2
 WIDE = 1024
 
 
@@ -97,11 +99,11 @@
         for c in range(chunks)
     ]
     wg_copies = [
-        pltpu.make_async_copy(wg_hbm.at[columns(c)], wg.at[columns(c)], w_sem.at[1, c])
+        pltpu.make_async_copy(wg_hbm.at[:, columns(c)], wg.at[:, columns(c)], w_sem.at[1, c])
         for c in range(chunks)
     ]
     wu_copies = [
-        pltpu.make_async_copy(wu_hbm.at[columns(c)], wu.at[columns(c)], w_sem.at[2, c])
+        pltpu.make_async_copy(wu_hbm.at[:, columns(c)], wu.at[:, columns(c)], w_sem.at[2, c])
         for c in range(chunks)
     ]
     wd_copies = [
@@ -212,7 +214,13 @@
         lhs[:, k * 128 : (k + 1) * 128] = att_wide[pl.ds(k, rows, stride=8), :].astype(BF16)
 
     half_rows, quarter_rows = n * 8, n * 4
-    group = (chunks + 6) // 7
+
+    def groups_of(count):
+        edges = [chunks * g // count for g in range(count + 1)]
+        return [(a, b - a) for a, b in zip(edges[:-1], edges[1:])]
+
+    rs_groups = groups_of(min(RS_GROUPS, chunks))
+    ag_groups = groups_of(min(AG_GROUPS, chunks))
 
     def move(src, dst, ssem, rsem, peer):
         return pltpu.make_async_remote_copy(
@@ -225,73 +233,84 @@
         )
 
     def reduce_rows(turn, product):
-        def to_twin(c):
+        def to_twin(g):
+            c, size = g
+            part_of = (turn, pl.ds(c, size))
             return move(
-                send1.at[turn, c], recv1.at[turn, c], s1_sem.at[turn, c], r1_sem.at[turn, c], twin
+                send1.at[part_of], recv1.at[part_of], s1_sem.at[turn, c], r1_sem.at[turn, c], twin
             )
 
-        def to_y(c):
+        def to_y(g):
+            c, size = g
+            part_of = (turn, pl.ds(c, size))
             return move(
-                send2.at[turn, c], recv2.at[turn, c], s2_sem.at[turn, c], r2_sem.at[turn, c], y_peer
+                send2.at[part_of], recv2.at[part_of], s2_sem.at[turn, c], r2_sem.at[turn, c], y_peer
             )
 
-        def to_z(c, off):
+        def to_z(g, off):
+            c, size = g
             other, peer = z_peer(off)
             return move(
-                send3.at[turn, c, other],
-                recv3.at[turn, c, off],
+                send3.at[turn, other, pl.ds(c, size)],
+                recv3.at[turn, off, pl.ds(c, size)],
                 s3_sem.at[turn, c, off],
                 r3_sem.at[turn, c, off],
                 peer,
             )
 
-        def first(c):
-            tile = product(c)
-            for j in range(8):
-                part[c, pl.ds(j, rows, stride=8), :] = tile[:, j * 128 : (j + 1) * 128]
+        def first(g):
             away = pl.multiple_of((1 - core) * half_rows, half_rows)
-            send1[turn, c] = part[c, pl.ds(away, half_rows), :].astype(BF16)
-            to_twin(c).start()
-
-        def second(c):
-            to_twin(c).wait_recv()
+            for c in range(g[0], g[0] + g[1]):
+                tile = product(c)
+                for j in range(8):
+                    part[c, pl.ds(j, rows, stride=8), :] = tile[:, j * 128 : (j + 1) * 128]
+                send1[turn, c] = part[c, pl.ds(away, half_rows), :].astype(BF16)
+            to_twin(g).start()
+
+        def second(g):
             home = pl.multiple_of(core * half_rows, half_rows)
-            acc1[c] = part[c, pl.ds(home, half_rows), :] + recv1[turn, c].astype(F32)
             away = pl.multiple_of((1 - y) * quarter_rows, quarter_rows)
-            send2[turn, c] = acc1[c, pl.ds(away, quarter_rows), :].astype(BF16)
-            to_y(c).start()
-
-        def third(c):
-            to_y(c).wait_recv()
+            to_twin(g).wait_recv()
+            for c in range(g[0], g[0] + g[1]):
+                acc1[c] = part[c, pl.ds(home, half_rows), :] + recv1[turn, c].astype(F32)
+                send2[turn, c] = acc1[c, pl.ds(away, quarter_rows), :].astype(BF16)
+            to_y(g).start()
+
+        def third(g):
             home = pl.multiple_of(y * quarter_rows, quarter_rows)
-            held = acc1[c, pl.ds(home, quarter_rows), :] + recv2[turn, c].astype(F32)
-            held = held.reshape(nz, 16, 128)
-            acc2[c] = held
-            send3[turn, c] = held.astype(BF16)
+            to_y(g).wait_recv()
+            for c in range(g[0], g[0] + g[1]):
+                held = acc1[c, pl.ds(home, quarter_rows), :] + recv2[turn, c].astype(F32)
+                held = held.reshape(nz, 16, 128)
+                acc2[c] = held
+                send3[turn, :, c] = held.astype(BF16)
             for off in range(1, nz):
-                to_z(c, off).start()
-
-        for step in range(chunks + 2):
-            if step < chunks:
-                first(step)
-            if 0 <= step - 1 < chunks:
-                second(step - 1)
-            if 0 <= step - 2 < chunks:
-                third(step - 2)
+                to_z(g, off).start()
+
+        count = len(rs_groups)
+        for step in range(count + 2):
+            if step < count:
+                first(rs_groups[step])
+            if 0 <= step - 1 < count:
+                second(rs_groups[step - 1])
+            if 0 <= step - 2 < count:
+                third(rs_groups[step - 2])
         sums = []
-        for c in range(chunks):
-            total = acc2[c, z]
+        for g in rs_groups:
             for off in range(1, nz):
-                to_z(c, off).wait_recv()
-                total = total + recv3[turn, c, off].astype(F32)
-            sums.append(total)
+                to_z(g, off).wait_recv()
+            for c in range(g[0], g[0] + g[1]):
+                total = acc2[c, z]
+                for off in range(1, nz):
+                    total = total + recv3[turn, off, c].astype(F32)
+                sums.append(total)
 
         def finish():
-            for c in range(chunks):
-                to_twin(c).wait_send()
-                to_y(c).wait_send()
+            for g in rs_groups:
+                to_twin(g).wait_send()
+                to_y(g).wait_send()
                 for off in range(1, nz):
-                    to_z(c, off).wait_send()
+                    to_z(g, off).wait_send()
 
         return sums, finish
 
@@ -317,54 +336,65 @@
     y_in_rows = pl.multiple_of((core * 2 + 1 - y) * quarter_rows, quarter_rows)
     core_in_rows = pl.multiple_of((1 - core) * half_rows, half_rows)
 
-    def spread_z(c, off):
-        block = rows_all.at[c, pl.ds(my_rows, 16)]
-        return move(block, block, gz_ssem.at[c, off], gz_rsem.at[c, off], z_peer(off)[1])
-
-    def landed_z(c, off):
+    def block_of_rows(g, start, size):
+        return rows_all.at[pl.ds(g[0], g[1]), pl.ds(start, size)]
+
+    def spread_z(g, off):
+        block = block_of_rows(g, my_rows, 16)
+        return move(block, block, gz_ssem.at[g[0], off], gz_rsem.at[g[0], off], z_peer(off)[1])
+
+    def landed_z(g, off):
         source = lax.rem(z + nz - off, nz)
-        block = rows_all.at[c, pl.ds(pl.multiple_of(y_rows + source * 16, 16), 16)]
-        return move(block, block, gz_ssem.at[c, off], gz_rsem.at[c, off], z_peer(off)[1])
-
-    def spread_y(c, start):
-        block = rows_all.at[c, pl.ds(start, quarter_rows)]
-        return move(block, block, gy_ssem.at[c], gy_rsem.at[c], y_peer)
-
-    def spread_core(c, start):
-        block = rows_all.at[c, pl.ds(start, half_rows)]
-        return move(block, block, gc_ssem.at[c], gc_rsem.at[c], twin)
-
-    for c in range(chunks):
-        gain = gain_ref[c].astype(F32)
-        gain = jnp.concatenate([gain, gain], axis=0)
-        rows_all[c, pl.ds(my_rows, 16), :] = (state[c] * scale * gain).astype(BF16)
+        block = block_of_rows(g, pl.multiple_of(y_rows + source * 16, 16), 16)
+        return move(block, block, gz_ssem.at[g[0], off], gz_rsem.at[g[0], off], z_peer(off)[1])
+
+    def spread_y(g, start):
+        block = block_of_rows(g, start, quarter_rows)
+        return move(block, block, gy_ssem.at[g[0]], gy_rsem.at[g[0]], y_peer)
+
+    def spread_core(g, start):
+        block = block_of_rows(g, start, half_rows)
+        return move(block, block, gc_ssem.at[g[0]], gc_rsem.at[g[0]], twin)
+
+    for g in ag_groups:
+        for c in range(g[0], g[0] + g[1]):
+            gain = gain_ref[c].astype(F32)
+            gain = jnp.concatenate([gain, gain], axis=0)
+            rows_all[c, pl.ds(my_rows, 16), :] = (state[c] * scale * gain).astype(BF16)
         for off in range(1, nz):
-            spread_z(c, off).start()
-
-    gate = jnp.zeros((rows, wg.shape[1]), F32)
-    up = jnp.zeros((rows, wg.shape[1]), F32)
-    for step in range(chunks + 2):
-        if step < chunks:
+            spread_z(g, off).start()
+
+    gate = jnp.zeros((rows, wg.shape[0]), F32)
+    up = jnp.zeros((rows, wg.shape[0]), F32)
+    count = len(ag_groups)
+    for step in range(count + 2):
+        if step < count:
+            g = ag_groups[step]
             for off in range(1, nz):
-                landed_z(step, off).wait_recv()
-            spread_y(step, y_rows).start()
-        if 0 <= step - 1 < chunks:
-            c = step - 1
-            spread_y(c, y_in_rows).wait_recv()
-            spread_core(c, core_rows).start()
-        if 0 <= step - 2 < chunks:
-            c = step - 2
-            spread_core(c, core_in_rows).wait_recv()
-            rows_wide[...] = rows_all[c].astype(F32)
-            for j in range(8):
-                normed[:, j * 128 : (j + 1) * 128] = rows_wide[
-                    pl.ds(j, rows, stride=8), :
-                ].astype(BF16)
-            held = normed[...]
-            wg_copies[c].wait()
-            wu_copies[c].wait()
-            gate = gate + jnp.dot(held, wg[columns(c), :], preferred_element_type=F32)
-            up = up + jnp.dot(held, wu[columns(c), :], preferred_element_type=F32)
+                landed_z(g, off).wait_recv()
+            spread_y(g, y_rows).start()
+        if 0 <= step - 1 < count:
+            g = ag_groups[step - 1]
+            spread_y(g, y_in_rows).wait_recv()
+            spread_core(g, core_rows).start()
+        if 0 <= step - 2 < count:
+            g = ag_groups[step - 2]
+            spread_core(g, core_in_rows).wait_recv()
+            for c in range(g[0], g[0] + g[1]):
+                rows_wide[...] = rows_all[c].astype(F32)
+                for j in range(8):
+                    normed[:, j * 128 : (j + 1) * 128] = rows_wide[
+                        pl.ds(j, rows, stride=8), :
+                    ].astype(BF16)
+                held = normed[...]
+                wg_copies[c].wait()
+                wu_copies[c].wait()
+                gate = gate + lax.dot_general(
+                    held, wg[:, columns(c)], contract_last, preferred_element_type=F32
+                )
+                up = up + lax.dot_general(
+                    held, wu[:, columns(c)], contract_last, preferred_element_type=F32
+                )
 
     hidden = (gate / (1.0 + jnp.exp(-gate)) * up).astype(BF16)
 
@@ -383,11 +413,11 @@
     lax.fori_loop(1, n, drain_att, 0)
     finish_first()
     finish_second()
-    for c in range(chunks):
+    for g in ag_groups:
         for off in range(1, nz):
-            spread_z(c, off).wait_send()
-        spread_y(c, y_rows).wait_send()
-        spread_core(c, core_rows).wait_send()
+            spread_z(g, off).wait_send()
+        spread_y(g, y_rows).wait_send()
+        spread_core(g, core_rows).wait_send()
 
 
 def per_device(
@@ -410,7 +440,6 @@
     heads_dev = head_count // n
     width = residual_in.shape[2]
     chunks = width // WIDE
-    units = gate_weight.shape[1]
     nz = n // 4
     positions = kv_pool.shape[0] * kv_pool.shape[1]
 
@@ -440,8 +469,8 @@
         scratch_shapes=[
             pltpu.VMEM((positions, 2 * head_width), BF16),
             pltpu.VMEM(out_weight.shape, BF16),
-            pltpu.VMEM(gate_weight.shape, BF16),
-            pltpu.VMEM(up_weight.shape, BF16),
+            pltpu.VMEM(gate_weight.shape[::-1], BF16),
+            pltpu.VMEM(up_weight.shape[::-1], BF16),
             pltpu.VMEM(down_weight.shape, BF16),
             pltpu.VMEM((n * 16, 128), F32),
             pltpu.VMEM((n, 16, 128), BF16),
@@ -455,8 +484,8 @@
             pltpu.VMEM((2, chunks, n * 4, 128), BF16),
             pltpu.VMEM((2, chunks, n * 4, 128), BF16),
             pltpu.VMEM((chunks, nz, 16, 128), F32),
-            pltpu.VMEM((2, chunks, nz, 16, 128), BF16),
-            pltpu.VMEM((2, chunks, nz, 16, 128), BF16),
+            pltpu.VMEM((2, nz, chunks, 16, 128), BF16),
+            pltpu.VMEM((2, nz, chunks, 16, 128), BF16),
             pltpu.VMEM((chunks, 16, 128), F32),
             pltpu.VMEM((chunks, n * 16, 128), BF16),
             pltpu.VMEM((n * 16, 128), F32),
@@ -496,8 +525,8 @@
         gain,
         cache,
         out_weight,
-        gate_weight,
-        up_weight,
+        gate_weight.T,
+        up_weight.T,
         down_weight,
     )
     return (

time: 108 us -> 66.9 us (0.62)
  local copies, waits for them, and re-layouts: 30.5 us -> 5.71 us
  Pallas kernels: 76.2 us -> 60.2 us
    unnamed x2 -> x0, local copies, waits for them, and re-layouts: 24.8 us -> none
    pallas_call x1, Pallas kernels: 76.2 us -> 60.2 us  [per_device(): pl.pallas_call(functools.partial(layer_kernel, n), out_shape=jax.ShapeDty...]
where the time goes in v2:
time: 66.9 us; the launch traced here: 66.5 us
  Pallas kernels  60.2 us (90%)
  local copies, waits for them, and re-layouts  5.71 us (9%)
  between operations  0.67 us (1%)
    pallas_call x1, Pallas kernels, per_device(): pl.pallas_call(functools.partial(layer_kernel, n), out_shape=jax.ShapeDty...  60.2 us
    transpose x1, local copies, waits for them, and re-layouts, per_device(): out.reshape(chunks, steps, 8, 128).transpose(1, 0, 2, 3)  1.45 us
    reshape x1, local copies, waits for them, and re-layouts, per_device(): residual = residual_in.reshape(steps, chunks, 8, 128).transpose(1, 0, 2,...  1.36 us

profile of v2, /device:TPU:0, one launch (start us, length us, event | category | flops | bytes accessed | tf_op | source)
XLA Modules:
  0.0 66.5 jit_solution(17730401392664589398)
XLA Ops:
  0.0 0.9 %reshape.27 = bf16[2,16,4,256]{3,2,1,0:T(4,128)(2,1)S(1)} reshape(bf16[2,1,16384]{2,0,1:T(2,128)(2,1)} %param.14) | data formatting | bytes 131072 | tf_op jit(solution)/shard_map/reshape | solution.py:447
  0.9 0.1 copy.20
  1.0 0.7 reshape.28.q_ref
  1.6 1.4 %copy_bitcast_fusion.2.res_ref = bf16[7,16,128]{2,1,0:T(8,128)(2,1)} fusion(bf16[1,2,56,128]{3,1,2,0:T(2,128)(2,1)} %bitcast.30), kind=kLoop, calls=%fused_computation.2 | loop fusion | bytes 57344 | tf_op jit(solution)/shard_map/reshape | solution.py:455
  3.0 1.3 %pad.4.fresh_ref = bf16[16,512]{1,0:T(8,128)(2,1)} pad(bf16[2,512]{1,0:T(2,128)(2,1)} %bitcast.32, bf16[]{:T(256)} %constant.2.clone.1), padding=0_14x0_0 | pad | bytes 18434 | tf_op jit(solution)/shard_map/jit(_pad)/pad | solution.py:451
  4.9 60.2 %decode_layer.1 = f32[7,16,128]{2,1,0:T(8,128)} custom-call(s32[1,24]{1,0:T(1,128)} %table_ref.1, s32[1]{0:T(128)S(6)} %copy.21.length_ref, bf16[128,256]{1,0:T(8,128)(2,1)} %reshape.28.q_ref, bf16[16,512]{1,0:T(8,128)(2,1)} %pad.4.fresh_ref, bf16[7,16,128]{2,1,0:T(8,128)(2,1)} %copy_bitcast_fusion.2.res_ref, bf16[7,8,128]{2,1,0:T(8,128)(2,1)} %bitcast.31, ...), custom_call_target="tpu_custom_call" | custom-call | flops 1262485504 | bytes 41025536 | tf_op jit(solution)/shard_map/decode_layer/pallas_call | solution.py:464
  65.1 1.4 %copy.14 = f32[2,7,8,128]{3,2,1,0:T(8,128)} copy(f32[2,7,8,128]{3,2,0,1:T(8,128)} %bitcast.29) | data formatting | bytes 114688 | tf_op jit(solution)/shard_map/transpose | solution.py:533

commit v3 on v2

--- a/solution.py
+++ b/solution.py
@@ -52,6 +52,9 @@
     rows_all,
     rows_wide,
     normed,
+    q_wide,
+    res,
+    fresh_wide,
     kv_sem,
     w_sem,
     att_ssem,
@@ -88,8 +91,10 @@
         other = lax.rem(z + off, nz)
         return other, other * 4 + y * 2 + core
 
-    kv_copy = pltpu.make_async_copy(kv_hbm, kv, kv_sem)
-    kv_copy.start()
+    key_copy = pltpu.make_async_copy(kv_hbm.at[:, :256], kv.at[:, :256], kv_sem.at[0])
+    value_copy = pltpu.make_async_copy(kv_hbm.at[:, 256:], kv.at[:, 256:], kv_sem.at[1])
+    key_copy.start()
+    value_copy.start()
 
     def columns(c):
         return pl.ds(c * WIDE, WIDE)
@@ -110,13 +115,6 @@
         pltpu.make_async_copy(wd_hbm.at[:, columns(c)], wd.at[:, columns(c)], w_sem.at[3, c])
         for c in range(chunks)
     ]
-    for copy in wo_copies:
-        copy.start()
-    for pair in zip(wg_copies, wu_copies):
-        for copy in pair:
-            copy.start()
-    for copy in wd_copies:
-        copy.start()
 
     barrier = pltpu.get_barrier_semaphore()
 
@@ -139,17 +137,29 @@
     position = order * block_rows + (place - block_of * block_rows)
     visible = position < length_ref[0]
 
-    q = q_ref[...]
+    for h in range(heads_dev):
+        for i in range(n):
+            at = (i * heads_dev + h) * 256
+            q_wide[pl.ds(h * rows + i * 2, 2), :] = q_ref[:, at : at + 256].astype(F32)
+    for c in range(chunks):
+        for j in range(8):
+            at = c * WIDE + j * 128
+            res[c, pl.ds(j, 2, stride=8), :] = res_ref[:, at : at + 128].astype(F32)
+    fresh_wide[...] = jnp.zeros_like(fresh_wide)
+    fresh_wide[pl.ds(0, 2), :] = fresh_ref[...].astype(F32)
+    q = q_wide[...].astype(BF16)
     q_rows = q.shape[0]
     contract_last = (((1,), (1,)), ((), ()))
-    fresh = fresh_ref[...]
+    fresh = fresh_wide[...].astype(BF16)
     fresh_scores = (
         lax.dot_general(q, fresh[:, :256], contract_last, preferred_element_type=F32) * 0.0625
     )
     step_of_row = lax.rem(lax.broadcasted_iota(jnp.int32, (q_rows, 16), 0), 2)
     fresh_step = lax.broadcasted_iota(jnp.int32, (q_rows, 16), 1)
     fresh_scores = jnp.where(fresh_step <= step_of_row, fresh_scores, -jnp.inf)
-    kv_copy.wait()
+    key_copy.wait()
+    for copy in wo_copies:
+        copy.start()
     scores = (
         lax.dot_general(q, kv[:, :256], contract_last, preferred_element_type=F32) * 0.0625
     )
@@ -162,6 +172,10 @@
     total = jnp.sum(weights, axis=1, keepdims=True) + jnp.sum(
         fresh_weights, axis=1, keepdims=True
     )
+    value_copy.wait()
+    for pair in zip(wg_copies, wu_copies):
+        for copy in pair:
+            copy.start()
     probs = (weights / total).astype(BF16)
     fresh_probs = (fresh_weights / total).astype(BF16)
     attended = jnp.dot(probs, kv[:, 256:], preferred_element_type=F32) + jnp.dot(
@@ -318,10 +332,12 @@
         wo_copies[c].wait()
         return jnp.dot(lhs[...], wo[:, columns(c)], preferred_element_type=F32)
 
+    for copy in wd_copies:
+        copy.start()
     sums, finish_first = reduce_rows(0, project)
     square = jnp.zeros((16, 128), F32)
     for c in range(chunks):
-        row = res_ref[c].astype(F32) + sums[c]
+        row = res[c] + sums[c]
         state[c] = row
         square = square + row * row
     scale0 = lax.rsqrt(jnp.sum(square[:8], keepdims=True) / width + 1e-06)
@@ -443,17 +459,9 @@
     nz = n // 4
     positions = kv_pool.shape[0] * kv_pool.shape[1]
 
-    q = (
-        queries.reshape(steps, n, heads_dev, head_width)
-        .transpose(2, 1, 0, 3)
-        .reshape(head_count * steps, head_width)
-    )
-    fresh = jnp.pad(new_kv.reshape(steps, -1), ((0, 16 - steps), (0, 0)))
-    residual = (
-        residual_in.reshape(steps, chunks, 8, 128)
-        .transpose(1, 0, 2, 3)
-        .reshape(chunks, 8 * steps, 128)
-    )
+    q = queries.reshape(steps, -1)
+    fresh = new_kv.reshape(steps, -1)
+    residual = residual_in.reshape(steps, -1)
     gain = norm_gain.reshape(chunks, 8, 128)
     cache = kv_pool.reshape(positions, 2 * head_width)
 
@@ -490,7 +498,10 @@
             pltpu.VMEM((chunks, n * 16, 128), BF16),
             pltpu.VMEM((n * 16, 128), F32),
             pltpu.VMEM((2 * n, WIDE), BF16),
-            dma(()),
+            pltpu.VMEM((head_count * steps, head_width), F32),
+            pltpu.VMEM((chunks, 16, 128), F32),
+            pltpu.VMEM((16, 2 * head_width), F32),
+            dma((2,)),
             dma((4, chunks)),
             dma((n,)),
             dma((n,)),

time: 66.9 us -> 52.9 us (0.79)
  Pallas kernels: 60.2 us -> 50.5 us
  local copies, waits for them, and re-layouts: 5.71 us -> 1.45 us
    pallas_call x1, Pallas kernels: 60.2 us -> 50.5 us  [per_device(): pl.pallas_call(functools.partial(layer_kernel, n), out_shape=jax.ShapeDty...]
    reshape x4 -> x0, local copies, waits for them, and re-layouts: 2.98 us -> none  [the longest x1 1.36 us: per_device(): residual = residual_in.reshape(steps, chunks, 8, 128).transpose(1, 0, 2,...]
    pad x1 -> x0, local copies, waits for them, and re-layouts: 1.28 us -> none  [per_device(): fresh = jnp.pad(new_kv.reshape(steps, -1), ((0, 16 - steps), (0, 0)))]
where the time goes in v3:
time: 52.9 us; the launch traced here: 52.6 us
  Pallas kernels  50.5 us (95%)
  local copies, waits for them, and re-layouts  1.45 us (3%)
  between operations  0.66 us (1%)
    pallas_call x1, Pallas kernels, per_device(): pl.pallas_call(functools.partial(layer_kernel, n), out_shape=jax.ShapeDty...  50.5 us
    transpose x1, local copies, waits for them, and re-layouts, per_device(): out.reshape(chunks, steps, 8, 128).transpose(1, 0, 2, 3)  1.45 us

profile of v3, /device:TPU:0, one launch (start us, length us, event | category | flops | bytes accessed | tf_op | source)
XLA Modules:
  0.0 52.6 jit_solution(13404199655622044149)
XLA Ops:
  0.7 50.5 %decode_layer.1 = f32[7,16,128]{2,1,0:T(8,128)} custom-call(s32[1,24]{1,0:T(1,128)} %table_ref.1, s32[1]{0:T(128)S(6)} %copy.13.length_ref, bf16[2,16384]{1,0:T(2,128)(2,1)} %bitcast.15, bf16[2,512]{1,0:T(2,128)(2,1)} %bitcast.18, bf16[2,7168]{1,0:T(2,128)(2,1)} %bitcast.16, bf16[7,8,128]{2,1,0:T(8,128)(2,1)} %bitcast.17, bf16[1536,512]{1,0:T(8,128)(2,1)} %bitcast.13, ...), custom_call_target="tpu_custom_call" | custom-call | flops 1262485504 | bytes 41025536 | tf_op jit(solution)/shard_map/decode_layer/pallas_call | solution.py:472
  51.2 1.4 %copy.12 = f32[2,7,8,128]{3,2,1,0:T(8,128)} copy(f32[2,7,8,128]{3,2,0,1:T(8,128)} %bitcast.14) | data formatting | bytes 114688 | tf_op jit(solution)/shard_map/transpose | solution.py:544

commit v4 on v3

--- a/solution.py
+++ b/solution.py
@@ -141,10 +141,6 @@
         for i in range(n):
             at = (i * heads_dev + h) * 256
             q_wide[pl.ds(h * rows + i * 2, 2), :] = q_ref[:, at : at + 256].astype(F32)
-    for c in range(chunks):
-        for j in range(8):
-            at = c * WIDE + j * 128
-            res[c, pl.ds(j, 2, stride=8), :] = res_ref[:, at : at + 128].astype(F32)
     fresh_wide[...] = jnp.zeros_like(fresh_wide)
     fresh_wide[pl.ds(0, 2), :] = fresh_ref[...].astype(F32)
     q = q_wide[...].astype(BF16)
@@ -173,11 +169,12 @@
         fresh_weights, axis=1, keepdims=True
     )
     value_copy.wait()
+    share = 1.0 / total
     for pair in zip(wg_copies, wu_copies):
         for copy in pair:
             copy.start()
-    probs = (weights / total).astype(BF16)
-    fresh_probs = (fresh_weights / total).astype(BF16)
+    probs = (weights * share).astype(BF16)
+    fresh_probs = (fresh_weights * share).astype(BF16)
     attended = jnp.dot(probs, kv[:, 256:], preferred_element_type=F32) + jnp.dot(
         fresh_probs, fresh[:, 256:], preferred_element_type=F32
     )
@@ -209,6 +206,10 @@
 
     lax.fori_loop(1, n, start_att, 0)
     att_recv[my_slot] = att_send[me]
+    for c in range(chunks):
+        for j in range(8):
+            at = c * WIDE + j * 128
+            res[c, pl.ds(j, 2, stride=8), :] = res_ref[:, at : at + 128].astype(F32)
 
     def wait_att(off, carry):
         source = slot_of(lax.rem(me + off, n))

time: 52.9 us -> 52.9 us (level)
  no operation moved by 1% of the time
where the time goes in v4:
time: 52.9 us; the launch traced here: 52.6 us
  Pallas kernels  50.5 us (95%)
  local copies, waits for them, and re-layouts  1.45 us (3%)
  between operations  0.66 us (1%)
    pallas_call x1, Pallas kernels, per_device(): pl.pallas_call(functools.partial(layer_kernel, n), out_shape=jax.ShapeDty...  50.5 us
    transpose x1, local copies, waits for them, and re-layouts, per_device(): out.reshape(chunks, steps, 8, 128).transpose(1, 0, 2, 3)  1.45 us

profile of v4, /device:TPU:0, one launch (start us, length us, event | category | flops | bytes accessed | tf_op | source)
XLA Modules:
  0.0 52.6 jit_solution(7169476181154081934)
XLA Ops:
  0.7 50.5 %decode_layer.1 = f32[7,16,128]{2,1,0:T(8,128)} custom-call(s32[1,24]{1,0:T(1,128)} %table_ref.1, s32[1]{0:T(128)S(6)} %copy.13.length_ref, bf16[2,16384]{1,0:T(2,128)(2,1)} %bitcast.15, bf16[2,512]{1,0:T(2,128)(2,1)} %bitcast.18, bf16[2,7168]{1,0:T(2,128)(2,1)} %bitcast.16, bf16[7,8,128]{2,1,0:T(8,128)(2,1)} %bitcast.17, bf16[1536,512]{1,0:T(8,128)(2,1)} %bitcast.13, ...), custom_call_target="tpu_custom_call" | custom-call | flops 1262485504 | bytes 41025536 | tf_op jit(solution)/shard_map/decode_layer/pallas_call | solution.py:473
  51.2 1.4 %copy.12 = f32[2,7,8,128]{3,2,1,0:T(8,128)} copy(f32[2,7,8,128]{3,2,0,1:T(8,128)} %bitcast.14) | data formatting | bytes 114688 | tf_op jit(solution)/shard_map/transpose | solution.py:545
